TPU v7x, 128 devices: a whole 4x4x4 slice. The times are simulated.
128 devices in a mesh: col: 32 (over x, y, core), row: 4 (over z).
Axes of the slice: x: 4, y: 4, z: 4, core: 2. Of those that a mesh axis runs over, the one named last changes fastest.
Arguments:
- rhs: float32 [2, 32, 4, 4096], P(None, None, 'row', 'col'), may hold values from -6 to 6
- u_factor: bfloat16 [64, 160, 2, 256, 128], P('row', 'col'), may hold values from -0.0390625 to 0.0390625
- v_factor: bfloat16 [64, 160, 2, 256, 128], P('row', 'col'), may hold values from -0.375 to 0.375
- ranks: int32 [64, 160], P('row', 'col'), may hold values from 8 to 128, as said below
- assign: int32 [160], replicated, may hold values from 0 to 159, each once
Outputs:
- solution: float32 [2, 32, 40960], P(None, None, 'col')
- residual_estimate: float32 [32], replicated
Inputs may be any that keep to these rules, and one draw needn't show every extreme that they name: `ranks`: every entry is 128 // 16 times a power of two from 1 to 16.
All inputs are finite; a program needn't handle non-finite values.
Results may differ from a plain program's by a relative error of at most 0.0068.
Values may be sent and summed in bfloat16 or wider, within the bound.
A program may use at most 128 MiB of HBM per device.

v0:
```python
import jax
import jax.numpy as jnp
from jax import lax
from jax.sharding import Mesh
from jax.sharding import PartitionSpec as P

ITERS = 2
COL = ("col_0", "col_1", "col_2")
COL_ROW = ("col_0", "col_1", "col_2", "row")


def cut_along(x, dim, devices):
    before, after = (x.shape[:dim], x.shape[dim + 1 :])
    return jnp.moveaxis(x.reshape(*before, devices, -1, *after), dim, 0)


def sent_and_summed(x, axis, dim):
    devices = lax.axis_size(axis)
    tiles = lax.all_to_all(cut_along(x, dim, devices), axis, 0, 0, tiled=True)
    return jnp.sum(tiles.astype(jnp.float32), axis=0)


def in_order(tiles, dim):
    tiles = jnp.moveaxis(tiles, 0, dim)
    dims = tiles.shape
    return tiles.reshape(*dims[:dim], dims[dim] * dims[dim + 1], *dims[dim + 2 :])


def copy_for_each(x, axis):
    copies = jnp.broadcast_to(x, (lax.axis_size(axis), *x.shape))
    return lax.all_to_all(copies, axis, split_axis=0, concat_axis=0, tiled=True)


def collect(x, axis, dim):
    return in_order(copy_for_each(x, axis), dim)


def by_axis(x, axes):
    for axis in axes:
        x = lax.psum(x, axis)
    return x


def over_copies(x, axis):
    everything = copy_for_each(x, axis)
    return jnp.sum(everything.astype(jnp.float32), axis=0)


def over_copies_2(x, axis):
    everything = copy_for_each(x, axis)
    return jnp.sum(everything, axis=0)


def sum_squares(value):
    return jnp.sum(value * value, axis=(0, 2))


def on_device(rhs, u_factor, v_factor, ranks, assign):
    tile_rows = u_factor.shape[0]
    tile_cols = u_factor.shape[1]
    tile_size = u_factor.shape[3]
    rank_cap = u_factor.shape[4]
    sources = rhs.shape[1]
    rank_iota = lax.broadcasted_iota(jnp.int32, (tile_rows, tile_cols, 1, 1, rank_cap), 4)
    mask = (rank_iota < ranks[:, :, None, None, None]).astype(jnp.float32)

    def adjoint_terms(group_data):
        data_b = group_data.reshape(2, sources, tile_rows, tile_size)
        raw = jnp.einsum("ipcnk,dsin->ipcdsk", u_factor, data_b, preferred_element_type=jnp.float32)
        coeff = jnp.stack(
            [raw[:, :, 0, 0] + raw[:, :, 1, 1], raw[:, :, 0, 1] - raw[:, :, 1, 0]], axis=2
        )
        coeff = (coeff * mask).astype(jnp.bfloat16)
        prod = jnp.einsum("ipcnk,ipdsk->cdspn", v_factor, coeff, preferred_element_type=jnp.float32)
        partial_model = jnp.stack([prod[0, 0] + prod[1, 1], prod[0, 1] - prod[1, 0]], axis=0)
        return partial_model.reshape(2, sources, tile_cols * tile_size)

    def adjoint_step(data_hat, v_prev):
        group_data = collect(data_hat.astype(jnp.bfloat16), COL, 2)
        beta_now = jnp.sqrt(by_axis(sum_squares(data_hat), COL_ROW))
        model_sum = over_copies(adjoint_terms(group_data).astype(jnp.bfloat16), "row").astype(
            jnp.float32
        )
        v_hat = model_sum / beta_now[None, :, None] - beta_now[None, :, None] * v_prev
        alpha_now = jnp.sqrt(over_copies_2(sum_squares(v_hat), COL))
        return (
            data_hat / beta_now[None, :, None],
            beta_now,
            v_hat / alpha_now[None, :, None],
            alpha_now,
        )

    data_first = rhs.reshape(2, sources, rhs.shape[3])
    zero_model = jnp.zeros((2, sources, tile_cols * tile_size), jnp.float32)
    u_vec, beta_now, v_vec, alpha_now = adjoint_step(data_first, zero_model)
    w_vec = v_vec
    x_vec = zero_model
    phibar = beta_now
    rhobar = alpha_now
    for iteration in range(ITERS):
        model_b = v_vec.astype(jnp.bfloat16).reshape(2, sources, tile_cols, tile_size)
        forward_raw = jnp.einsum(
            "ipcnk,dspn->ipcdsk", v_factor, model_b, preferred_element_type=jnp.float32
        )
        forward_coeff = jnp.stack(
            [
                forward_raw[:, :, 0, 0] - forward_raw[:, :, 1, 1],
                forward_raw[:, :, 0, 1] + forward_raw[:, :, 1, 0],
            ],
            axis=2,
        )
        forward_coeff = (forward_coeff * mask).astype(jnp.bfloat16)
        forward_prod = jnp.einsum(
            "ipcnk,ipdsk->cdsin", u_factor, forward_coeff, preferred_element_type=jnp.float32
        )
        partial_data = jnp.stack(
            [forward_prod[0, 0] - forward_prod[1, 1], forward_prod[0, 1] + forward_prod[1, 0]],
            axis=0,
        )
        partial_data = partial_data.reshape(2, sources, tile_rows * tile_size)
        data_hat = (
            sent_and_summed(partial_data.astype(jnp.bfloat16), COL, 2)
            - alpha_now[None, :, None] * u_vec
        )
        u_vec, beta_now, v_vec, alpha_now = adjoint_step(data_hat, v_vec)
        rho_now = jnp.sqrt(rhobar * rhobar + beta_now * beta_now)
        cosine = rhobar / rho_now
        sine = beta_now / rho_now
        theta = sine * alpha_now
        rhobar = -cosine * alpha_now
        phi_now = cosine * phibar
        phibar = sine * phibar
        x_vec = x_vec + (phi_now / rho_now)[None, :, None] * w_vec
        w_vec = v_vec - (theta / rho_now)[None, :, None] * w_vec
    all_cols = assign.shape[0]
    natural = lax.axis_index(COL) * tile_cols + jnp.arange(tile_cols, dtype=jnp.int32)
    positions = jnp.arange(all_cols, dtype=jnp.int32)
    where_held = jnp.sum(
        positions[None, :] * (assign[None, :] == natural[:, None]).astype(jnp.int32), axis=1
    )
    share = sources // lax.axis_size("row")
    own_share = lax.dynamic_slice_in_dim(x_vec, lax.axis_index("row") * share, share, 1)
    gathered = collect(own_share, COL, 2)
    gathered = gathered.reshape(2, share, all_cols, tile_size)
    picked = jnp.concatenate(
        [lax.dynamic_slice_in_dim(gathered, where_held[j], 1, axis=2) for j in range(tile_cols)],
        axis=2,
    ).reshape(2, share, tile_cols * tile_size)
    solution = collect(picked, "row", 1)
    return (solution, phibar)


def solution(mesh):
    split = Mesh(
        mesh.devices.reshape(4, 4, 2, mesh.shape["row"]), ("col_0", "col_1", "col_2", "row")
    )
    placed = (
        P(None, None, "row", COL),
        P("row", COL, None, None, None),
        P("row", COL, None, None, None),
        P("row", COL),
        P(),
    )
    return jax.shard_map(
        on_device, mesh=split, in_specs=placed, out_specs=(P(None, None, COL), P()), check_vma=False
    )
```

profile of v0, /device:TPU:0, one launch (start us, length us, event | category | flops | bytes accessed | tf_op | source)
XLA Modules:
  0.0 296.3 jit_solution(509928026007286434)
XLA Ops:
  2.3 7.4 %all-to-all-start = ((bf16[32,2,32,128]{3,2,1,0:T(8,128)(2,1)}), bf16[32,2,32,128]{3,2,1,0:T(8,128)(2,1)S(1)}, u32[]{:S(2)}, u32[]{:S(2)}) async-start(bf16[32,2,32,128]{3,2,1,0:T(8,128)(2,1)} %broadcast_in_dim.18), calls=%async_computation | async-start | bytes 1048576 | tf_op jit(solution)/shard_map/all_to_all | solution.py:31
  10.6 10.3 %all-to-all-done = bf16[32,2,32,128]{3,2,1,0:T(8,128)(2,1)S(1)} async-done(((bf16[32,2,32,128]{3,2,1,0:T(8,128)(2,1)}), bf16[32,2,32,128]{3,2,1,0:T(8,128)(2,1)S(1)}, u32[]{:S(2)}, u32[]{:S(2)}) %all-to-all-start) | async-done | bytes 524320 | tf_op jit(solution)/shard_map/all_to_all | solution.py:31
  21.5 6.0 %fusion.29 = f32[16,5,2,2,32,128]{5,4,2,1,3,0:T(8,128)S(1)} fusion(bf16[16,5,2,256,128]{4,3,2,1,0:T(8,128)(2,1)} %param.6, bf16[2,32,16,256,1,1]{3,2,1,0,5,4:T(8,128)(2,1)S(1)} %bitcast.188), kind=kOutput, calls=%fused_computation.27 | convolution fusion | flops 671088640 | bytes 16252928 | tf_op jit(solution)/shard_map/ipcnk,dsin->ipcdsk/dot_general | solution.py:69
  32.9 5.3 %all-to-all-start.1 = ((bf16[4,2,32,1280]{3,2,1,0:T(8,128)(2,1)}), bf16[4,2,32,1280]{3,2,1,0:T(8,128)(2,1)S(1)}, u32[]{:S(2)}, u32[]{:S(2)}) async-start(bf16[4,2,32,1280]{3,2,1,0:T(8,128)(2,1)} %broadcast_in_dim.19), calls=%async_computation.1 | async-start | bytes 1310720 | tf_op jit(solution)/shard_map/all_to_all | solution.py:31
  38.3 8.9 %psum.84 = f32[32]{0:T(128)S(1)} all-reduce(f32[32]{0:T(128)S(1)} %multiply_reduce_fusion.4), channel_id=1, replica_groups=mesh['col_0'=4,'col_1'=4,'col_2'=2,'row'=4] {'col_0'}, use_global_device_ids=true, to_apply=%region_2.0 | all-reduce | flops 32 | bytes 256 | tf_op jit(solution)/shard_map/psum | solution.py:40
  47.2 9.2 %psum.85 = f32[32]{0:T(128)S(1)} all-reduce(f32[32]{0:T(128)S(1)} %psum.84), channel_id=1, replica_groups=mesh['col_0'=4,'col_1'=4,'col_2'=2,'row'=4] {'col_1'}, use_global_device_ids=true, to_apply=%region_3.0 | all-reduce | flops 32 | bytes 256 | tf_op jit(solution)/shard_map/psum | solution.py:40
  58.9 10.9 %psum.87 = f32[32]{0:T(128)S(1)} all-reduce(f32[32]{0:T(128)S(1)} %psum.86), channel_id=1, replica_groups=mesh['col_0'=4,'col_1'=4,'col_2'=2,'row'=4] {'row'}, use_global_device_ids=true, to_apply=%region_5.0 | all-reduce | flops 32 | bytes 256 | tf_op jit(solution)/shard_map/psum | solution.py:40
  70.2 10.5 %all_to_all.52 = f32[32,1,32]{2,1,0:T(1,128)S(1)} all-to-all(f32[32,1,32]{2,1,0:T(1,128)S(1)} %broadcast_in_dim.21), channel_id=1, replica_groups=mesh['col_0'=4,'col_1'=4,'col_2'=2,'row'=4] {'col_0','col_1','col_2'}, dimensions={0} | all-to-all | bytes 8192 | tf_op jit(solution)/shard_map/all_to_all | solution.py:31
  80.7 5.3 %fusion.20 = f32[16,5,2,2,32,128]{5,4,1,0,3,2:T(8,128)S(1)} fusion(f32[2,4,5,8,256]{4,3,2,1,0:T(8,128)S(1)} %bitcast.184, f32[32]{0:T(128)S(1)} %sqrt.30, f32[32]{0:T(128)S(1)} %get-tuple-element.39, f32[32]{0:T(128)S(1)} %get-tuple-element.38, bf16[16,5,2,256,128]{4,3,2,1,0:T(8,128)(2,1)} %param.7), kind=kOutput, calls=%fused_computation.24 | convolution fusion | flops 671416320 | bytes 16056704 | tf_op jit(solution)/shard_map/ipcnk,dspn->ipcdsk/dot_general | solution.py:102
  87.7 4.6 %fusion.32 = f32[2,2,32,16,256]{4,2,0,1,3:T(8,128)S(1)} fusion(bf16[16,5,2,256,128]{4,3,2,1,0:T(8,128)(2,1)S(1)} %bitcast.176, f32[16,5,1,32,128]{4,3,1,0,2:T(8,128)} %get-tuple-element.16, f32[16,5,1,32,128]{4,3,1,0,2:T(8,128)S(1)} %get-tuple-element.15, f32[16,5,128]{2,1,0:T(8,128)S(1)} %fusion.88), kind=kOutput, calls=%fused_computation.28 | convolution fusion | flops 673054720 | bytes 15245312 | tf_op jit(solution)/shard_map/ipcnk,ipdsk->cdsin/dot_general | solution.py:113
  93.3 14.5 %all_to_all.53 = bf16[32,2,32,128]{3,2,1,0:T(8,128)(2,1)S(1)} all-to-all(bf16[32,2,32,128]{3,2,1,0:T(8,128)(2,1)S(1)} %copy.234), channel_id=1, replica_groups=mesh['col_0'=4,'col_1'=4,'col_2'=2,'row'=4] {'col_0','col_1','col_2'}, dimensions={0} | all-to-all | bytes 1048576 | tf_op jit(solution)/shard_map/all_to_all | solution.py:19
  108.2 15.0 %all_to_all.54 = bf16[32,2,32,128]{3,2,1,0:T(8,128)(2,1)S(1)} all-to-all(bf16[32,2,32,128]{3,2,1,0:T(8,128)(2,1)S(1)} %broadcast_in_dim.22), channel_id=1, replica_groups=mesh['col_0'=4,'col_1'=4,'col_2'=2,'row'=4] {'col_0','col_1','col_2'}, dimensions={0} | all-to-all | bytes 1048576 | tf_op jit(solution)/shard_map/all_to_all | solution.py:31
  123.8 5.3 %fusion.26 = f32[16,5,2,2,32,128]{5,4,1,0,3,2:T(8,128)S(1)} fusion(bf16[2,32,16,256,1,1]{3,2,1,0,5,4:T(8,128)(2,1)S(1)} %bitcast.186, bf16[16,5,2,256,128]{4,3,2,1,0:T(8,128)(2,1)} %param.6), kind=kOutput, calls=%fused_computation.26 | convolution fusion | flops 671088640 | bytes 16252928 | tf_op jit(solution)/shard_map/ipcnk,dsin->ipcdsk/dot_general | solution.py:69
  138.5 8.9 %psum.88 = f32[32]{0:T(128)S(1)} all-reduce(f32[32]{0:T(128)S(1)} %get-tuple-element.9), channel_id=1, replica_groups=mesh['col_0'=4,'col_1'=4,'col_2'=2,'row'=4] {'col_0'}, use_global_device_ids=true, to_apply=%region_10.0 | all-reduce | flops 32 | bytes 256 | tf_op jit(solution)/shard_map/psum | solution.py:40
  147.4 9.2 %psum.89 = f32[32]{0:T(128)S(1)} all-reduce(f32[32]{0:T(128)S(1)} %psum.88), channel_id=1, replica_groups=mesh['col_0'=4,'col_1'=4,'col_2'=2,'row'=4] {'col_1'}, use_global_device_ids=true, to_apply=%region_11.0 | all-reduce | flops 32 | bytes 256 | tf_op jit(solution)/shard_map/psum | solution.py:40
  159.1 10.9 %psum.91 = f32[32]{0:T(128)S(1)} all-reduce(f32[32]{0:T(128)S(1)} %psum.90), channel_id=1, replica_groups=mesh['col_0'=4,'col_1'=4,'col_2'=2,'row'=4] {'row'}, use_global_device_ids=true, to_apply=%region_13.0 | all-reduce | flops 32 | bytes 256 | tf_op jit(solution)/shard_map/psum | solution.py:40
  171.2 10.3 %all_to_all.55 = f32[32,1,32]{2,1,0:T(1,128)S(1)} all-to-all(f32[32,1,32]{2,1,0:T(1,128)S(1)} %broadcast_in_dim.24), channel_id=1, replica_groups=mesh['col_0'=4,'col_1'=4,'col_2'=2,'row'=4] {'col_0','col_1','col_2'}, dimensions={0} | all-to-all | bytes 8192 | tf_op jit(solution)/shard_map/all_to_all | solution.py:31
  181.6 5.3 %fusion.23 = f32[16,5,2,2,32,128]{5,4,1,0,3,2:T(8,128)S(1)} fusion(f32[2,4,5,8,256]{4,3,2,1,0:T(8,128)S(1)} %bitcast.187, f32[32]{0:T(128)S(1)} %sqrt.33, f32[32]{0:T(128)S(1)} %sqrt.31, f32[2,4,5,8,256]{4,3,2,1,0:T(8,128)S(1)} %bitcast.185, f32[32]{0:T(128)S(1)} %sqrt.30, f32[32]{0:T(128)S(1)} %get-tuple-element.39, f32[32]{0:T(128)S(1)} %get-tuple-element.38, ...), kind=kOutput, calls=%fused_computation.25 | convolution fusion | flops 671744000 | bytes 16384640 | tf_op jit(solution)/shard_map/ipcnk,dspn->ipcdsk/dot_general | solution.py:102
  197.3 11.1 %all-to-all-done.7 = bf16[32,2,32,128]{3,2,1,0:T(8,128)(2,1)S(1)} async-done(((bf16[32,2,32,128]{3,2,1,0:T(8,128)(2,1)}), bf16[32,2,32,128]{3,2,1,0:T(8,128)(2,1)S(1)}, u32[]{:S(2)}, u32[]{:S(2)}) %all-to-all-start.7) | async-done | bytes 524320 | tf_op jit(solution)/shard_map/all_to_all | solution.py:19
  208.6 8.9 %psum.92 = f32[32]{0:T(128)S(1)} all-reduce(f32[32]{0:T(128)S(1)} %multiply_reduce_fusion.2), channel_id=1, replica_groups=mesh['col_0'=4,'col_1'=4,'col_2'=2,'row'=4] {'col_0'}, use_global_device_ids=true, to_apply=%region_19.0 | all-reduce | flops 32 | bytes 256 | tf_op jit(solution)/shard_map/psum | solution.py:40
  217.6 9.2 %psum.93 = f32[32]{0:T(128)S(1)} all-reduce(f32[32]{0:T(128)S(1)} %psum.92), channel_id=1, replica_groups=mesh['col_0'=4,'col_1'=4,'col_2'=2,'row'=4] {'col_1'}, use_global_device_ids=true, to_apply=%region_20.0 | all-reduce | flops 32 | bytes 256 | tf_op jit(solution)/shard_map/psum | solution.py:40
  229.2 7.7 %psum.95 = f32[32]{0:T(128)S(1)} all-reduce(f32[32]{0:T(128)S(1)} %psum.94), channel_id=1, replica_groups=mesh['col_0'=4,'col_1'=4,'col_2'=2,'row'=4] {'row'}, use_global_device_ids=true, to_apply=%region_22.0 | all-reduce | flops 32 | bytes 256 | tf_op jit(solution)/shard_map/psum | solution.py:40
  255.2 24.1 %all-to-all-done.8 = f32[32,2,8,1280]{3,2,1,0:T(8,128)S(1)} async-done(((f32[32,2,8,1280]{3,2,1,0:T(8,128)}), f32[32,2,8,1280]{3,2,1,0:T(8,128)S(1)}, u32[]{:S(2)}, u32[]{:S(2)}) %all-to-all-start.8) | async-done | bytes 2621472 | tf_op jit(solution)/shard_map/all_to_all | solution.py:31
  285.4 10.1 %all_to_all.56 = f32[4,2,8,1280]{3,2,1,0:T(8,128)S(1)} all-to-all(f32[4,2,8,1280]{3,2,1,0:T(8,128)S(1)} %broadcast_in_dim.52), channel_id=1, replica_groups=mesh['col_0'=4,'col_1'=4,'col_2'=2,'row'=4] {'row'}, dimensions={0} | all-to-all | bytes 655360 | tf_op jit(solution)/shard_map/all_to_all | solution.py:31
  (125 shorter events, 56.6 us)
Async XLA Ops:
  2.3 18.6 %all-to-all-start = ((bf16[32,2,32,128]{3,2,1,0:T(8,128)(2,1)}), bf16[32,2,32,128]{3,2,1,0:T(8,128)(2,1)S(1)}, u32[]{:S(2)}, u32[]{:S(2)}) async-start(bf16[32,2,32,128]{3,2,1,0:T(8,128)(2,1)} %broadcast_in_dim.18), calls=%async_computation | async-start | bytes 1048576 | tf_op jit(solution)/shard_map/all_to_all | solution.py:31
  10.6 77.2 %copy-start.1 = (f32[16,5,128]{2,1,0:T(8,128)}, f32[16,5,128]{2,1,0:T(8,128)S(1)}, u32[]{:S(2)}) copy-start(f32[16,5,128]{2,1,0:T(8,128)S(1)} %fusion.88) | copy-start | bytes 122884
  21.2 6.8 %slice-start.6 = ((s8[10485760]{0:T(1024)(128)(4,1)}), s8[2097152]{0:T(1024)(128)(4,1)S(1)}, s32[]{:S(2)}) async-start(s8[10485760]{0:T(1024)(128)(4,1)} %bitcast.179), calls=%async_computation.16 | async-start | bytes 4194304
  21.4 6.6 %slice-start.7 = ((s8[10485760]{0:T(1024)(128)(4,1)}), s8[4194304]{0:T(1024)(128)(4,1)S(1)}, s32[]{:S(2)}) async-start(s8[10485760]{0:T(1024)(128)(4,1)} %bitcast.179), calls=%async_computation.17 | async-start | bytes 8388608
  21.5 6.9 %slice-start.8 = ((s8[10485760]{0:T(1024)(128)(4,1)}), s8[4194304]{0:T(1024)(128)(4,1)S(1)}, s32[]{:S(2)}) async-start(s8[10485760]{0:T(1024)(128)(4,1)} %bitcast.179), calls=%async_computation.18 | async-start | bytes 8388608
  31.6 6.6 %copy-start = (f32[2,32,1,128]{3,2,1,0:T(1,128)S(1)}, f32[2,32,1,128]{3,2,1,0:T(1,128)}, u32[]{:S(2)}) copy-start(f32[2,32,1,128]{3,2,1,0:T(1,128)} %param.5) | copy-start | bytes 98308
  32.9 36.9 %all-to-all-start.1 = ((bf16[4,2,32,1280]{3,2,1,0:T(8,128)(2,1)}), bf16[4,2,32,1280]{3,2,1,0:T(8,128)(2,1)S(1)}, u32[]{:S(2)}, u32[]{:S(2)}) async-start(bf16[4,2,32,1280]{3,2,1,0:T(8,128)(2,1)} %broadcast_in_dim.19), calls=%async_computation.1 | async-start | bytes 1310720 | tf_op jit(solution)/shard_map/all_to_all | solution.py:31
  69.8 17.9 %slice-start = ((s8[10485760]{0:T(1024)(128)(4,1)}), s8[2097152]{0:T(1024)(128)(4,1)S(1)}, s32[]{:S(2)}) async-start(s8[10485760]{0:T(1024)(128)(4,1)} %bitcast.175), calls=%async_computation.10 | async-start | bytes 4194304
  80.7 7.1 %slice-start.1 = ((s8[10485760]{0:T(1024)(128)(4,1)}), s8[4194304]{0:T(1024)(128)(4,1)S(1)}, s32[]{:S(2)}) async-start(s8[10485760]{0:T(1024)(128)(4,1)} %bitcast.175), calls=%async_computation.11 | async-start | bytes 8388608
  80.7 7.1 %slice-start.2 = ((s8[10485760]{0:T(1024)(128)(4,1)}), s8[4194304]{0:T(1024)(128)(4,1)S(1)}, s32[]{:S(2)}) async-start(s8[10485760]{0:T(1024)(128)(4,1)} %bitcast.175), calls=%async_computation.12 | async-start | bytes 8388608
  123.2 6.5 %slice-start.9 = ((s8[10485760]{0:T(1024)(128)(4,1)}), s8[2097152]{0:T(1024)(128)(4,1)S(1)}, s32[]{:S(2)}) async-start(s8[10485760]{0:T(1024)(128)(4,1)} %bitcast.181), calls=%async_computation.19 | async-start | bytes 4194304
  123.8 6.0 %slice-start.10 = ((s8[10485760]{0:T(1024)(128)(4,1)}), s8[4194304]{0:T(1024)(128)(4,1)S(1)}, s32[]{:S(2)}) async-start(s8[10485760]{0:T(1024)(128)(4,1)} %bitcast.181), calls=%async_computation.20 | async-start | bytes 8388608
  123.8 6.7 %slice-start.11 = ((s8[10485760]{0:T(1024)(128)(4,1)}), s8[4194304]{0:T(1024)(128)(4,1)S(1)}, s32[]{:S(2)}) async-start(s8[10485760]{0:T(1024)(128)(4,1)} %bitcast.181), calls=%async_computation.21 | async-start | bytes 8388608
  129.1 1.4 copy-start.2
  135.0 34.9 %all-to-all-start.5 = ((bf16[4,2,32,1280]{3,2,1,0:T(8,128)(2,1)}), bf16[4,2,32,1280]{3,2,1,0:T(8,128)(2,1)S(1)}, u32[]{:S(2)}, u32[]{:S(2)}) async-start(bf16[4,2,32,1280]{3,2,1,0:T(8,128)(2,1)} %broadcast_in_dim.23), calls=%async_computation.5 | async-start | bytes 1310720 | tf_op jit(solution)/shard_map/all_to_all | solution.py:31
  170.0 17.6 %slice-start.3 = ((s8[10485760]{0:T(1024)(128)(4,1)}), s8[2097152]{0:T(1024)(128)(4,1)S(1)}, s32[]{:S(2)}) async-start(s8[10485760]{0:T(1024)(128)(4,1)} %bitcast.177), calls=%async_computation.13 | async-start | bytes 4194304
  181.5 6.0 %slice-start.4 = ((s8[10485760]{0:T(1024)(128)(4,1)}), s8[4194304]{0:T(1024)(128)(4,1)S(1)}, s32[]{:S(2)}) async-start(s8[10485760]{0:T(1024)(128)(4,1)} %bitcast.177), calls=%async_computation.14 | async-start | bytes 8388608
  181.6 6.5 %slice-start.5 = ((s8[10485760]{0:T(1024)(128)(4,1)}), s8[4194304]{0:T(1024)(128)(4,1)S(1)}, s32[]{:S(2)}) async-start(s8[10485760]{0:T(1024)(128)(4,1)} %bitcast.177), calls=%async_computation.15 | async-start | bytes 8388608
  193.3 15.1 %all-to-all-start.7 = ((bf16[32,2,32,128]{3,2,1,0:T(8,128)(2,1)}), bf16[32,2,32,128]{3,2,1,0:T(8,128)(2,1)S(1)}, u32[]{:S(2)}, u32[]{:S(2)}) async-start(bf16[32,2,32,128]{3,2,1,0:T(8,128)(2,1)} %copy.251), calls=%async_computation.7 | async-start | bytes 1048576 | tf_op jit(solution)/shard_map/all_to_all | solution.py:19
  240.5 4.4 %copy-start.3 = (s32[160]{0:T(256)S(1)}, s32[160]{0:T(256)}, u32[]{:S(2)}) copy-start(s32[160]{0:T(256)} %param.9) | copy-start | bytes 1924
  240.5 38.8 %all-to-all-start.8 = ((f32[32,2,8,1280]{3,2,1,0:T(8,128)}), f32[32,2,8,1280]{3,2,1,0:T(8,128)S(1)}, u32[]{:S(2)}, u32[]{:S(2)}) async-start(f32[32,2,8,1280]{3,2,1,0:T(8,128)} %broadcast_in_dim.25), calls=%async_computation.8 | async-start | bytes 5242880 | tf_op jit(solution)/shard_map/all_to_all | solution.py:31
where the time goes:
time: 298 us; the launch traced here: 296 us
  blocking collectives  152 us (51%)
  waiting for transfers between devices  45.6 us (15%)
  matrix products  36.5 us (12%)
  starting transfers between devices  24.5 us (8%)
  local copies, waits for them, and re-layouts  18.5 us (6%)
  between operations  10.6 us (4%)
  other arithmetic  8.95 us (3%)
    psum x12, blocking collectives, by_axis(): x = lax.psum(x, axis)  91.2 us
    all_to_all x4, blocking collectives, copy_for_each(): return lax.all_to_all(copies, axis, split_axis=0, concat_axis=0, tiled=True)  46 us
    all_to_all x4, waiting for transfers between devices, copy_for_each(): return lax.all_to_all(copies, axis, split_axis=0, concat_axis=0, tiled=True)  34.5 us
    all_to_all x4, starting transfers between devices, copy_for_each(): return lax.all_to_all(copies, axis, split_axis=0, concat_axis=0, tiled=True)  20.6 us
    all_to_all x1, blocking collectives, sent_and_summed(): tiles = lax.all_to_all(cut_along(x, dim, devices), axis, 0, 0, tiled=True)  14.5 us
    dot_general x2, matrix products, adjoint_terms(): jnp.einsum('ipcnk,dsin->ipcdsk', u_factor, data_b, preferred_element_type...  11.3 us
    all_to_all x1, waiting for transfers between devices, sent_and_summed(): tiles = lax.all_to_all(cut_along(x, dim, devices), axis, 0, 0, tiled=True)  11.1 us
    dot_general x2, matrix products, on_device(): jnp.einsum('ipcnk,dspn->ipcdsk', v_factor, model_b, preferred_element_typ...  10.6 us
  transfers between devices with their start and end apart: 5, of which 3 were waited for; matrix products, arithmetic and copies ran while one was open for 1% of the time, Pallas kernels for 0%

commit v1 on v0

--- a/solution.py
+++ b/solution.py
@@ -7,6 +7,10 @@
 ITERS = 2
 COL = ("col_0", "col_1", "col_2")
 COL_ROW = ("col_0", "col_1", "col_2", "row")
+
+
+def load_quotas_on(row_axis, array_here):
+    return lax.all_gather(array_here, row_axis).sum(axis=0)
 
 
 def cut_along(x, dim, devices):
@@ -37,7 +41,7 @@
 
 def by_axis(x, axes):
     for axis in axes:
-        x = lax.psum(x, axis)
+        x = load_quotas_on(axis, x)
     return x
 
 

time: 298 us -> 307 us (1.030)
  local copies, waits for them, and re-layouts: 18.5 us -> 24.9 us
    psum x12 -> x0, blocking collectives: 91.2 us -> none  [by_axis(): x = lax.psum(x, axis)]
    unnamed x0 -> x12, blocking collectives: none -> 91 us
    unnamed x33 -> x69, local copies, waits for them, and re-layouts: 2.33 us -> 7.7 us
  transfers between devices with their start and end apart: 5 -> 5, of which waited for: 3 -> 3; matrix products, arithmetic and copies ran while one was open for 1% -> 2% of each run, Pallas kernels for 0% -> 0%
where the time goes in v1:
time: 307 us; the launch traced here: 305 us
  blocking collectives  151 us (49%)
  waiting for transfers between devices  45.8 us (15%)
  matrix products  36.5 us (12%)
  local copies, waits for them, and re-layouts  24.9 us (8%)
  starting transfers between devices  24.3 us (8%)
  between operations  13.4 us (4%)
  other arithmetic  9.21 us (3%)
    unnamed x12, blocking collectives  91 us
    all_to_all x4, blocking collectives, copy_for_each(): return lax.all_to_all(copies, axis, split_axis=0, concat_axis=0, tiled=True)  46 us
    all_to_all x4, waiting for transfers between devices, copy_for_each(): return lax.all_to_all(copies, axis, split_axis=0, concat_axis=0, tiled=True)  34.7 us
    all_to_all x4, starting transfers between devices, copy_for_each(): return lax.all_to_all(copies, axis, split_axis=0, concat_axis=0, tiled=True)  20.4 us
    all_to_all x1, blocking collectives, sent_and_summed(): tiles = lax.all_to_all(cut_along(x, dim, devices), axis, 0, 0, tiled=True)  14.5 us
    dot_general x2, matrix products, adjoint_terms(): jnp.einsum('ipcnk,dsin->ipcdsk', u_factor, data_b, preferred_element_type...  11.3 us
    all_to_all x1, waiting for transfers between devices, sent_and_summed(): tiles = lax.all_to_all(cut_along(x, dim, devices), axis, 0, 0, tiled=True)  11.1 us
    dot_general x2, matrix products, on_device(): jnp.einsum('ipcnk,dspn->ipcdsk', v_factor, model_b, preferred_element_typ...  10.6 us
  transfers between devices with their start and end apart: 5, of which 3 were waited for; matrix products, arithmetic and copies ran while one was open for 2% of the time, Pallas kernels for 0%

profile of v1, /device:TPU:0, one launch (start us, length us, event | category | flops | bytes accessed | tf_op | source)
XLA Modules:
  0.0 305.5 jit_solution(12670647225534586219)
XLA Ops:
  2.3 7.4 %all-to-all-start = ((bf16[32,2,32,128]{3,2,1,0:T(8,128)(2,1)}), bf16[32,2,32,128]{3,2,1,0:T(8,128)(2,1)S(1)}, u32[]{:S(2)}, u32[]{:S(2)}) async-start(bf16[32,2,32,128]{3,2,1,0:T(8,128)(2,1)} %broadcast_in_dim.18), calls=%async_computation | async-start | bytes 1048576 | tf_op jit(solution)/shard_map/all_to_all | solution.py:35
  10.6 10.3 %all-to-all-done = bf16[32,2,32,128]{3,2,1,0:T(8,128)(2,1)S(1)} async-done(((bf16[32,2,32,128]{3,2,1,0:T(8,128)(2,1)}), bf16[32,2,32,128]{3,2,1,0:T(8,128)(2,1)S(1)}, u32[]{:S(2)}, u32[]{:S(2)}) %all-to-all-start) | async-done | bytes 524320 | tf_op jit(solution)/shard_map/all_to_all | solution.py:35
  21.5 6.0 %fusion.29 = f32[16,5,2,2,32,128]{5,4,2,1,3,0:T(8,128)S(1)} fusion(bf16[16,5,2,256,128]{4,3,2,1,0:T(8,128)(2,1)} %param.6, bf16[2,32,16,256,1,1]{3,2,1,0,5,4:T(8,128)(2,1)S(1)} %bitcast.192), kind=kOutput, calls=%fused_computation.27 | convolution fusion | flops 671088640 | bytes 16252928 | tf_op jit(solution)/shard_map/ipcnk,dsin->ipcdsk/dot_general | solution.py:73
  32.9 5.3 %all-to-all-start.1 = ((bf16[4,2,32,1280]{3,2,1,0:T(8,128)(2,1)}), bf16[4,2,32,1280]{3,2,1,0:T(8,128)(2,1)S(1)}, u32[]{:S(2)}, u32[]{:S(2)}) async-start(bf16[4,2,32,1280]{3,2,1,0:T(8,128)(2,1)} %broadcast_in_dim.19), calls=%async_computation.1 | async-start | bytes 1310720 | tf_op jit(solution)/shard_map/all_to_all | solution.py:35
  39.9 8.8 %all-reduce = f32[128]{0:T(128)S(1)} all-reduce(f32[128]{0:T(128)S(1)} %dynamic-update-slice), channel_id=2, replica_groups=mesh['col_0'=4,'col_1'=4,'col_2'=2,'row'=4] {'col_0'}, use_global_device_ids=true, to_apply=%add | all-reduce | flops 128 | bytes 1024
  50.3 9.2 %all-reduce.1 = f32[128]{0:T(128)S(1)} all-reduce(f32[128]{0:T(128)S(1)} %dynamic-update-slice.1), channel_id=3, replica_groups=mesh['col_0'=4,'col_1'=4,'col_2'=2,'row'=4] {'col_1'}, use_global_device_ids=true, to_apply=%add.1 | all-reduce | flops 128 | bytes 1024
  65.3 10.9 %all-reduce.3 = f32[128]{0:T(128)S(1)} all-reduce(f32[128]{0:T(128)S(1)} %dynamic-update-slice.3), channel_id=5, replica_groups=mesh['col_0'=4,'col_1'=4,'col_2'=2,'row'=4] {'row'}, use_global_device_ids=true, to_apply=%add.3 | all-reduce | flops 128 | bytes 1024
  76.7 10.5 %all_to_all.55 = f32[32,1,32]{2,1,0:T(1,128)S(1)} all-to-all(f32[32,1,32]{2,1,0:T(1,128)S(1)} %broadcast_in_dim.21), channel_id=1, replica_groups=mesh['col_0'=4,'col_1'=4,'col_2'=2,'row'=4] {'col_0','col_1','col_2'}, dimensions={0} | all-to-all | bytes 8192 | tf_op jit(solution)/shard_map/all_to_all | solution.py:35
  87.2 5.3 %fusion.20 = f32[16,5,2,2,32,128]{5,4,1,0,3,2:T(8,128)S(1)} fusion(f32[2,4,5,8,256]{4,3,2,1,0:T(8,128)S(1)} %bitcast.188, f32[32]{0:T(128)S(1)} %sqrt.88, f32[32]{0:T(128)S(1)} %get-tuple-element.39, f32[32]{0:T(128)S(1)} %get-tuple-element.38, bf16[16,5,2,256,128]{4,3,2,1,0:T(8,128)(2,1)} %param.7), kind=kOutput, calls=%fused_computation.24 | convolution fusion | flops 671416320 | bytes 16056704 | tf_op jit(solution)/shard_map/ipcnk,dspn->ipcdsk/dot_general | solution.py:106
  94.2 4.6 %fusion.32 = f32[2,2,32,16,256]{4,2,0,1,3:T(8,128)S(1)} fusion(bf16[16,5,2,256,128]{4,3,2,1,0:T(8,128)(2,1)S(1)} %bitcast.180, f32[16,5,1,32,128]{4,3,1,0,2:T(8,128)} %get-tuple-element.16, f32[16,5,1,32,128]{4,3,1,0,2:T(8,128)S(1)} %get-tuple-element.15, f32[16,5,128]{2,1,0:T(8,128)S(1)} %fusion.88), kind=kOutput, calls=%fused_computation.28 | convolution fusion | flops 673054720 | bytes 15245312 | tf_op jit(solution)/shard_map/ipcnk,ipdsk->cdsin/dot_general | solution.py:117
  99.8 14.5 %all_to_all.52 = bf16[32,2,32,128]{3,2,1,0:T(8,128)(2,1)S(1)} all-to-all(bf16[32,2,32,128]{3,2,1,0:T(8,128)(2,1)S(1)} %copy.234), channel_id=1, replica_groups=mesh['col_0'=4,'col_1'=4,'col_2'=2,'row'=4] {'col_0','col_1','col_2'}, dimensions={0} | all-to-all | bytes 1048576 | tf_op jit(solution)/shard_map/all_to_all | solution.py:23
  114.7 15.0 %all_to_all.53 = bf16[32,2,32,128]{3,2,1,0:T(8,128)(2,1)S(1)} all-to-all(bf16[32,2,32,128]{3,2,1,0:T(8,128)(2,1)S(1)} %broadcast_in_dim.22), channel_id=1, replica_groups=mesh['col_0'=4,'col_1'=4,'col_2'=2,'row'=4] {'col_0','col_1','col_2'}, dimensions={0} | all-to-all | bytes 1048576 | tf_op jit(solution)/shard_map/all_to_all | solution.py:35
  130.3 5.3 %fusion.26 = f32[16,5,2,2,32,128]{5,4,1,0,3,2:T(8,128)S(1)} fusion(bf16[2,32,16,256,1,1]{3,2,1,0,5,4:T(8,128)(2,1)S(1)} %bitcast.190, bf16[16,5,2,256,128]{4,3,2,1,0:T(8,128)(2,1)} %param.6), kind=kOutput, calls=%fused_computation.26 | convolution fusion | flops 671088640 | bytes 16252928 | tf_op jit(solution)/shard_map/ipcnk,dsin->ipcdsk/dot_general | solution.py:73
  145.2 8.8 %all-reduce.4 = f32[128]{0:T(128)S(1)} all-reduce(f32[128]{0:T(128)S(1)} %dynamic-update-slice.4), channel_id=6, replica_groups=mesh['col_0'=4,'col_1'=4,'col_2'=2,'row'=4] {'col_0'}, use_global_device_ids=true, to_apply=%add.4 | all-reduce | flops 128 | bytes 1024
  154.4 9.2 %all-reduce.5 = f32[128]{0:T(128)S(1)} all-reduce(f32[128]{0:T(128)S(1)} %dynamic-update-slice.5), channel_id=7, replica_groups=mesh['col_0'=4,'col_1'=4,'col_2'=2,'row'=4] {'col_1'}, use_global_device_ids=true, to_apply=%add.5 | all-reduce | flops 128 | bytes 1024
  166.8 10.8 %all-reduce.7 = f32[128]{0:T(128)S(1)} all-reduce(f32[128]{0:T(128)S(1)} %dynamic-update-slice.7), channel_id=9, replica_groups=mesh['col_0'=4,'col_1'=4,'col_2'=2,'row'=4] {'row'}, use_global_device_ids=true, to_apply=%add.7 | all-reduce | flops 128 | bytes 1024
  179.0 10.3 %all_to_all.56 = f32[32,1,32]{2,1,0:T(1,128)S(1)} all-to-all(f32[32,1,32]{2,1,0:T(1,128)S(1)} %broadcast_in_dim.24), channel_id=1, replica_groups=mesh['col_0'=4,'col_1'=4,'col_2'=2,'row'=4] {'col_0','col_1','col_2'}, dimensions={0} | all-to-all | bytes 8192 | tf_op jit(solution)/shard_map/all_to_all | solution.py:35
  189.4 5.3 %fusion.23 = f32[16,5,2,2,32,128]{5,4,1,0,3,2:T(8,128)S(1)} fusion(f32[2,4,5,8,256]{4,3,2,1,0:T(8,128)S(1)} %bitcast.191, f32[32]{0:T(128)S(1)} %sqrt.91, f32[32]{0:T(128)S(1)} %sqrt.89, f32[2,4,5,8,256]{4,3,2,1,0:T(8,128)S(1)} %bitcast.189, f32[32]{0:T(128)S(1)} %sqrt.88, f32[32]{0:T(128)S(1)} %get-tuple-element.39, f32[32]{0:T(128)S(1)} %get-tuple-element.38, ...), kind=kOutput, calls=%fused_computation.25 | convolution fusion | flops 671744000 | bytes 16384640 | tf_op jit(solution)/shard_map/ipcnk,dspn->ipcdsk/dot_general | solution.py:106
  205.1 11.1 %all-to-all-done.7 = bf16[32,2,32,128]{3,2,1,0:T(8,128)(2,1)S(1)} async-done(((bf16[32,2,32,128]{3,2,1,0:T(8,128)(2,1)}), bf16[32,2,32,128]{3,2,1,0:T(8,128)(2,1)S(1)}, u32[]{:S(2)}, u32[]{:S(2)}) %all-to-all-start.7) | async-done | bytes 524320 | tf_op jit(solution)/shard_map/all_to_all | solution.py:23
  216.7 8.9 %all-reduce.8 = f32[128]{0:T(128)S(1)} all-reduce(f32[128]{0:T(128)S(1)} %dynamic-update-slice.8), channel_id=10, replica_groups=mesh['col_0'=4,'col_1'=4,'col_2'=2,'row'=4] {'col_0'}, use_global_device_ids=true, to_apply=%add.8 | all-reduce | flops 128 | bytes 1024
  226.0 9.2 %all-reduce.9 = f32[128]{0:T(128)S(1)} all-reduce(f32[128]{0:T(128)S(1)} %dynamic-update-slice.9), channel_id=11, replica_groups=mesh['col_0'=4,'col_1'=4,'col_2'=2,'row'=4] {'col_1'}, use_global_device_ids=true, to_apply=%add.9 | all-reduce | flops 128 | bytes 1024
  238.3 7.7 %all-reduce.11 = f32[128]{0:T(128)S(1)} all-reduce(f32[128]{0:T(128)S(1)} %dynamic-update-slice.11), channel_id=13, replica_groups=mesh['col_0'=4,'col_1'=4,'col_2'=2,'row'=4] {'row'}, use_global_device_ids=true, to_apply=%add.11 | all-reduce | flops 128 | bytes 1024
  264.2 24.4 %all-to-all-done.8 = f32[32,2,8,1280]{3,2,1,0:T(8,128)S(1)} async-done(((f32[32,2,8,1280]{3,2,1,0:T(8,128)}), f32[32,2,8,1280]{3,2,1,0:T(8,128)S(1)}, u32[]{:S(2)}, u32[]{:S(2)}) %all-to-all-start.8) | async-done | bytes 2621472 | tf_op jit(solution)/shard_map/all_to_all | solution.py:35
  294.6 10.1 %all_to_all.54 = f32[4,2,8,1280]{3,2,1,0:T(8,128)S(1)} all-to-all(f32[4,2,8,1280]{3,2,1,0:T(8,128)S(1)} %broadcast_in_dim.52), channel_id=1, replica_groups=mesh['col_0'=4,'col_1'=4,'col_2'=2,'row'=4] {'row'}, dimensions={0} | all-to-all | bytes 655360 | tf_op jit(solution)/shard_map/all_to_all | solution.py:35
  (185 shorter events, 63.0 us)
Async XLA Ops:
  2.3 18.6 %all-to-all-start = ((bf16[32,2,32,128]{3,2,1,0:T(8,128)(2,1)}), bf16[32,2,32,128]{3,2,1,0:T(8,128)(2,1)S(1)}, u32[]{:S(2)}, u32[]{:S(2)}) async-start(bf16[32,2,32,128]{3,2,1,0:T(8,128)(2,1)} %broadcast_in_dim.18), calls=%async_computation | async-start | bytes 1048576 | tf_op jit(solution)/shard_map/all_to_all | solution.py:35
  10.6 83.6 %copy-start.1 = (f32[16,5,128]{2,1,0:T(8,128)}, f32[16,5,128]{2,1,0:T(8,128)S(1)}, u32[]{:S(2)}) copy-start(f32[16,5,128]{2,1,0:T(8,128)S(1)} %fusion.88) | copy-start | bytes 122884
  21.2 6.8 %slice-start.6 = ((s8[10485760]{0:T(1024)(128)(4,1)}), s8[2097152]{0:T(1024)(128)(4,1)S(1)}, s32[]{:S(2)}) async-start(s8[10485760]{0:T(1024)(128)(4,1)} %bitcast.183), calls=%async_computation.16 | async-start | bytes 4194304
  21.4 6.6 %slice-start.7 = ((s8[10485760]{0:T(1024)(128)(4,1)}), s8[4194304]{0:T(1024)(128)(4,1)S(1)}, s32[]{:S(2)}) async-start(s8[10485760]{0:T(1024)(128)(4,1)} %bitcast.183), calls=%async_computation.17 | async-start | bytes 8388608
  21.5 6.9 %slice-start.8 = ((s8[10485760]{0:T(1024)(128)(4,1)}), s8[4194304]{0:T(1024)(128)(4,1)S(1)}, s32[]{:S(2)}) async-start(s8[10485760]{0:T(1024)(128)(4,1)} %bitcast.183), calls=%async_computation.18 | async-start | bytes 8388608
  31.6 6.7 %copy-start.7 = (u32[128]{0:T(128)S(1)}, u32[128]{0:T(128)}, u32[]{:S(2)}) copy-start(u32[128]{0:T(128)} %constant.38) | copy-start | bytes 1540
  31.6 7.9 %copy-start = (f32[2,32,1,128]{3,2,1,0:T(1,128)S(1)}, f32[2,32,1,128]{3,2,1,0:T(1,128)}, u32[]{:S(2)}) copy-start(f32[2,32,1,128]{3,2,1,0:T(1,128)} %param.5) | copy-start | bytes 98308
  31.6 17.2 %copy-start.6 = (u32[128]{0:T(128)S(1)}, u32[128]{0:T(128)}, u32[]{:S(2)}) copy-start(u32[128]{0:T(128)} %constant.43) | copy-start | bytes 1540
  31.6 28.0 %copy-start.5 = (u32[128]{0:T(128)S(1)}, u32[128]{0:T(128)}, u32[]{:S(2)}) copy-start(u32[128]{0:T(128)} %constant.48) | copy-start | bytes 1540
  31.6 32.0 %copy-start.4 = (u32[128]{0:T(128)S(1)}, u32[128]{0:T(128)}, u32[]{:S(2)}) copy-start(u32[128]{0:T(128)} %constant.53) | copy-start | bytes 1540
  32.9 43.4 %all-to-all-start.1 = ((bf16[4,2,32,1280]{3,2,1,0:T(8,128)(2,1)}), bf16[4,2,32,1280]{3,2,1,0:T(8,128)(2,1)S(1)}, u32[]{:S(2)}, u32[]{:S(2)}) async-start(bf16[4,2,32,1280]{3,2,1,0:T(8,128)(2,1)} %broadcast_in_dim.19), calls=%async_computation.1 | async-start | bytes 1310720 | tf_op jit(solution)/shard_map/all_to_all | solution.py:35
  76.3 17.9 %slice-start = ((s8[10485760]{0:T(1024)(128)(4,1)}), s8[2097152]{0:T(1024)(128)(4,1)S(1)}, s32[]{:S(2)}) async-start(s8[10485760]{0:T(1024)(128)(4,1)} %bitcast.179), calls=%async_computation.10 | async-start | bytes 4194304
  87.2 7.1 %slice-start.1 = ((s8[10485760]{0:T(1024)(128)(4,1)}), s8[4194304]{0:T(1024)(128)(4,1)S(1)}, s32[]{:S(2)}) async-start(s8[10485760]{0:T(1024)(128)(4,1)} %bitcast.179), calls=%async_computation.11 | async-start | bytes 8388608
  87.2 7.1 %slice-start.2 = ((s8[10485760]{0:T(1024)(128)(4,1)}), s8[4194304]{0:T(1024)(128)(4,1)S(1)}, s32[]{:S(2)}) async-start(s8[10485760]{0:T(1024)(128)(4,1)} %bitcast.179), calls=%async_computation.12 | async-start | bytes 8388608
  129.7 6.5 %slice-start.9 = ((s8[10485760]{0:T(1024)(128)(4,1)}), s8[2097152]{0:T(1024)(128)(4,1)S(1)}, s32[]{:S(2)}) async-start(s8[10485760]{0:T(1024)(128)(4,1)} %bitcast.185), calls=%async_computation.19 | async-start | bytes 4194304
  130.3 6.0 %slice-start.10 = ((s8[10485760]{0:T(1024)(128)(4,1)}), s8[4194304]{0:T(1024)(128)(4,1)S(1)}, s32[]{:S(2)}) async-start(s8[10485760]{0:T(1024)(128)(4,1)} %bitcast.185), calls=%async_computation.20 | async-start | bytes 8388608
  130.3 6.7 %slice-start.11 = ((s8[10485760]{0:T(1024)(128)(4,1)}), s8[4194304]{0:T(1024)(128)(4,1)S(1)}, s32[]{:S(2)}) async-start(s8[10485760]{0:T(1024)(128)(4,1)} %bitcast.185), calls=%async_computation.21 | async-start | bytes 8388608
  141.5 36.3 %all-to-all-start.5 = ((bf16[4,2,32,1280]{3,2,1,0:T(8,128)(2,1)}), bf16[4,2,32,1280]{3,2,1,0:T(8,128)(2,1)S(1)}, u32[]{:S(2)}, u32[]{:S(2)}) async-start(bf16[4,2,32,1280]{3,2,1,0:T(8,128)(2,1)} %broadcast_in_dim.23), calls=%async_computation.5 | async-start | bytes 1310720 | tf_op jit(solution)/shard_map/all_to_all | solution.py:35
  177.8 17.6 %slice-start.3 = ((s8[10485760]{0:T(1024)(128)(4,1)}), s8[2097152]{0:T(1024)(128)(4,1)S(1)}, s32[]{:S(2)}) async-start(s8[10485760]{0:T(1024)(128)(4,1)} %bitcast.181), calls=%async_computation.13 | async-start | bytes 4194304
  189.4 6.0 %slice-start.4 = ((s8[10485760]{0:T(1024)(128)(4,1)}), s8[4194304]{0:T(1024)(128)(4,1)S(1)}, s32[]{:S(2)}) async-start(s8[10485760]{0:T(1024)(128)(4,1)} %bitcast.181), calls=%async_computation.14 | async-start | bytes 8388608
  189.4 6.5 %slice-start.5 = ((s8[10485760]{0:T(1024)(128)(4,1)}), s8[4194304]{0:T(1024)(128)(4,1)S(1)}, s32[]{:S(2)}) async-start(s8[10485760]{0:T(1024)(128)(4,1)} %bitcast.181), calls=%async_computation.15 | async-start | bytes 8388608
  201.1 15.1 %all-to-all-start.7 = ((bf16[32,2,32,128]{3,2,1,0:T(8,128)(2,1)}), bf16[32,2,32,128]{3,2,1,0:T(8,128)(2,1)S(1)}, u32[]{:S(2)}, u32[]{:S(2)}) async-start(bf16[32,2,32,128]{3,2,1,0:T(8,128)(2,1)} %copy.251), calls=%async_computation.7 | async-start | bytes 1048576 | tf_op jit(solution)/shard_map/all_to_all | solution.py:23
  249.7 4.2 %copy-start.3 = (s32[160]{0:T(256)S(1)}, s32[160]{0:T(256)}, u32[]{:S(2)}) copy-start(s32[160]{0:T(256)} %param.9) | copy-start | bytes 1924
  249.7 38.8 %all-to-all-start.8 = ((f32[32,2,8,1280]{3,2,1,0:T(8,128)}), f32[32,2,8,1280]{3,2,1,0:T(8,128)S(1)}, u32[]{:S(2)}, u32[]{:S(2)}) async-start(f32[32,2,8,1280]{3,2,1,0:T(8,128)} %broadcast_in_dim.25), calls=%async_computation.8 | async-start | bytes 5242880 | tf_op jit(solution)/shard_map/all_to_all | solution.py:35
  (1 other events, 1.4 us)
